TPU v7x, 32 devices: a whole 2x2x4 slice. The times are simulated.
32 devices in a mesh: grp: 8 (over y, x, core), mem: 4 (over z).
Axes of the slice: x: 2, y: 2, z: 4, core: 2. Of those that a mesh axis runs over, the one named last changes fastest.
Arguments:
- incident: bfloat16 [2, 256, 16384], P(None, None, ('grp', 'mem')), may hold values from -6 to 6
- near_blocks: bfloat16 [64, 3, 2, 256, 256], P(('grp', 'mem')), may hold values from -0.15625 to 0.15625
- near_mask: int32 [64, 3], P(('grp', 'mem')), may hold values 0 or 1
- far_source: int32 [8, 14], replicated, may hold values from 0 to 7
- far_rank: int32 [8, 14], P('grp'), may hold values from 32 to 128
- basis_in: bfloat16 [8, 4, 14, 2, 128, 512], P('grp', 'mem'), may hold values from -0.1875 to 0.1875
- section_one: bfloat16 [8, 4, 14, 2, 128, 256], P('grp', 'mem'), may hold values from -0.25 to 0.25
- section_two: bfloat16 [8, 4, 14, 2, 128, 256], P('grp', 'mem'), may hold values from -0.25 to 0.25
- basis_out: bfloat16 [8, 4, 14, 2, 2048, 128], P('grp', 'mem'), may hold values from -0.0625 to 0.0625
Outputs:
- product: bfloat16 [2, 256, 16384], P(None, None, ('grp', 'mem'))
Inputs may be any that keep to these rules, and one draw needn't show every extreme that they name: far_source names the cluster whose coefficients feed each far-field block; clusters may repeat. far_rank gives the number of live rank components of each block. `near_mask`: 1 marks a present near-field block.
All inputs are finite; a program needn't handle non-finite values.
Results may differ from a plain program's by a relative error of at most 0.0053.
Values may be sent and summed in bfloat16 or wider, within the bound.
A program may use at most 128 MiB of HBM per device.

v0:
```python
import jax
import jax.numpy as jnp
from jax import lax
from jax.sharding import PartitionSpec as P


def with_halo(block, sides, width):
    for axis, dim in sides:
        count = lax.axis_size(axis)
        forward = [(i, i + 1) for i in range(count - 1)]
        backward = [(target, source) for source, target in forward]
        low = lax.ppermute(
            lax.slice_in_dim(block, block.shape[dim] - width, None, axis=dim), axis, forward
        )
        high = lax.ppermute(lax.slice_in_dim(block, 0, width, axis=dim), axis, backward)
        block = jnp.concatenate([low, block, high], axis=dim)
    return block


def partner_2(value, axis, stride):
    return lax.ppermute(value, axis, [(i, i ^ 1 << stride) for i in range(lax.axis_size(axis))])


def complex_apply(weight_real, weight_imag, vector_real, vector_imag, form):

    def mult(left, right):
        return jnp.einsum(form, left, right, preferred_element_type=jnp.float32)

    first = mult(weight_real, vector_real) - mult(weight_imag, vector_imag)
    second = mult(weight_real, vector_imag) + mult(weight_imag, vector_real)
    return (first, second)


def mix_section(level, partner, upper_bit, weights, keep):
    is_upper = upper_bit == 1
    lower_half = jnp.where(is_upper, partner, level)
    upper_half = jnp.where(is_upper, level, partner)
    joined = jnp.concatenate([lower_half, upper_half], -1)
    first, second = complex_apply(
        weights[:, 0], weights[:, 1], joined[:, 0], joined[:, 1], "fkj,fnj->fnk"
    )
    return jnp.stack([first * keep, second * keep], 1).astype(jnp.bfloat16)


def on_device(
    incident,
    near_blocks,
    near_mask,
    far_source,
    far_rank,
    basis_in,
    section_one,
    section_two,
    basis_out,
):
    nrhs_count = incident.shape[1]
    row_count = incident.shape[2]
    leaf_size = near_blocks.shape[3]
    leaf_count = near_blocks.shape[0]
    rank_size = basis_in.shape[4]
    group = lax.axis_index("grp")
    member = lax.axis_index("mem")
    sources = lax.dynamic_slice_in_dim(far_source, group, 1, 0)[0]
    arrived = lax.all_gather(incident[None], "grp", axis=0, tiled=True)
    chosen = jnp.take(arrived, sources, axis=0)
    padded = with_halo(incident, ((("grp", "mem"), 2),), leaf_size)
    near_real = jnp.zeros((nrhs_count, leaf_count, leaf_size), jnp.float32)
    near_imag = jnp.zeros((nrhs_count, leaf_count, leaf_size), jnp.float32)
    for offset in range(3):
        window = padded[:, :, offset * leaf_size : offset * leaf_size + row_count].reshape(
            2, nrhs_count, leaf_count, leaf_size
        )
        first, second = complex_apply(
            near_blocks[:, offset, 0],
            near_blocks[:, offset, 1],
            window[0],
            window[1],
            "lab,nlb->nla",
        )
        weight = near_mask[:, offset].astype(jnp.float32)[None, :, None]
        near_real = near_real + weight * first
        near_imag = near_imag + weight * second
    near = jnp.stack(
        [near_real.reshape(nrhs_count, row_count), near_imag.reshape(nrhs_count, row_count)], 0
    )
    keep = (jnp.arange(rank_size)[None, :] < far_rank[0][:, None]).astype(jnp.float32)[:, None, :]
    factor = basis_in[0, 0]
    first, second = complex_apply(
        factor[:, 0], factor[:, 1], chosen[:, 0], chosen[:, 1], "fkr,fnr->fnk"
    )
    level = jnp.stack([first * keep, second * keep], 1).astype(jnp.bfloat16)
    partner = partner_2(level, "mem", 0)
    level = mix_section(level, partner, member % 2, section_one[0, 0], keep)
    partner = partner_2(level, "mem", 1)
    level = mix_section(level, partner, member // 2 % 2, section_two[0, 0], keep)
    outward = basis_out[0, 0]
    first, second = complex_apply(
        outward[:, 0], outward[:, 1], level[:, 0], level[:, 1], "frk,fnk->nr"
    )
    terms = jnp.stack([first, second], 0)
    far = lax.psum_scatter(terms, "mem", scatter_dimension=2, tiled=True)
    return (far + near).astype(jnp.bfloat16)


def solution(mesh):
    placed = (
        P(None, None, ("grp", "mem")),
        P(("grp", "mem"), None, None, None, None),
        P(("grp", "mem"), None),
        P(),
        P("grp", None),
        P("grp", "mem", None, None, None, None),
        P("grp", "mem", None, None, None, None),
        P("grp", "mem", None, None, None, None),
        P("grp", "mem", None, None, None, None),
    )
    return jax.shard_map(
        on_device,
        mesh=mesh,
        in_specs=placed,
        out_specs=P(None, None, ("grp", "mem")),
        check_vma=False,
    )
```

profile of v0, /device:TPU:0, one launch (start us, length us, event | category | flops | bytes accessed | tf_op | source)
XLA Modules:
  0.0 305.5 jit_solution(6309968522782846975)
XLA Ops:
  7.3 4.3 %copy.174 = bf16[1,1,14,2,128,512]{5,4,2,3,1,0:T(8,128)(2,1)} copy(bf16[1,1,14,2,128,512]{5,4,3,2,1,0:T(8,128)(2,1)} %param.14) | data formatting | bytes 7340032 | tf_op args[5]
  13.1 35.6 %all-gather.3.cloned.1.call-done = bf16[16,256,512]{2,1,0:T(8,128)(2,1)} async-done(((bf16[2,256,512]{2,1,0:T(8,128)(2,1)}), bf16[16,256,512]{2,1,0:T(8,128)(2,1)}) %all-gather.3.cloned.1.call-update) | async-done | bytes 4194320 | tf_op jit(solution)/shard_map/all_gather | solution.py:64
  48.7 6.6 %gather_fusion = bf16[14,2,256,512]{3,2,1,0:T(8,128)(2,1)} fusion(bf16[8,2,256,512]{3,2,1,0:T(8,128)(2,1)} %bitcast.218, s32[1024]{0:T(1024)S(1)} %pad_clamp_fusion), kind=kCustom, calls=%fused_computation | custom fusion | bytes 14680120 | tf_op jit(solution)/shard_map/jit(_take)/gather | solution.py:65
  55.3 4.0 %copy_select_fusion = bf16[14,2,256,512]{3,2,0,1:T(8,128)(2,1)S(1)} fusion(bf16[14,2,256,512]{3,2,1,0:T(8,128)(2,1)} %gather_fusion, pred[14]{0:T(512)(128)(4,1)S(1)} %compare_and_fusion), kind=kLoop, calls=%fused_computation.4 | loop fusion | flops 3670016 | bytes 14680078 | tf_op jit(solution)/shard_map/jit(_take)/select_n | solution.py:65
  62.1 1.5 fusion.23
  63.6 1.5 fusion.22
  68.1 1.7 copy.176
  69.8 39.3 %collective-permute-done = bf16[14,2,256,128]{2,3,0,1:T(8,128)(2,1)} collective-permute-done((bf16[14,2,256,128]{2,3,0,1:T(8,128)(2,1)}, bf16[14,2,256,128]{2,3,0,1:T(8,128)(2,1)}, u32[]{:S(2)}, u32[]{:S(2)}) %collective-permute-start) | collective-permute-done | bytes 1835040 | tf_op jit(solution)/shard_map/ppermute | solution.py:21
  109.1 1.7 broadcast_select_fusion
  114.5 2.4 collective-permute-start.1
  116.9 1.7 copy.175
  118.6 7.3 %copy.173 = bf16[1,1,14,2,2048,128]{5,4,2,3,1,0:T(8,128)(2,1)S(1)} copy(bf16[1,1,14,2,2048,128]{5,4,3,2,1,0:T(8,128)(2,1)} %param.17) | data formatting | bytes 29360128 | tf_op args[8]
  125.9 70.5 %collective-permute-done.1 = bf16[14,2,256,128]{2,3,0,1:T(8,128)(2,1)} collective-permute-done((bf16[14,2,256,128]{2,3,0,1:T(8,128)(2,1)}, bf16[14,2,256,128]{2,3,0,1:T(8,128)(2,1)}, u32[]{:S(2)}, u32[]{:S(2)}) %collective-permute-start.1) | collective-permute-done | bytes 1835040 | tf_op jit(solution)/shard_map/ppermute | solution.py:21
  196.4 1.7 broadcast_select_fusion.3
  200.5 2.1 fusion.9
  202.6 2.1 fusion.8
  204.8 2.1 fusion.13
  206.9 2.1 fusion.15
  209.0 2.2 pad_maximum_fusion
  214.0 4.6 %collective-permute-start.2 = (bf16[2,256,256]{1,2,0:T(8,128)(2,1)S(1)}, bf16[2,256,256]{1,2,0:T(8,128)(2,1)S(1)}, u32[]{:S(2)}, u32[]{:S(2)}) collective-permute-start(bf16[2,256,256]{1,2,0:T(8,128)(2,1)S(1)} %get-tuple-element.21), channel_id=1, source_target_pairs={{0,1},{1,2},{2,3},{3,4},{4,5},{5,6},{6,7},{7,8},{8,9},{9,10},{10,1... | collective-permute-start | bytes 786440 | tf_op jit(solution)/shard_map/ppermute | solution.py:12
  218.8 11.6 %collective-permute-done.3 = bf16[2,256,256]{1,2,0:T(8,128)(2,1)S(1)} collective-permute-done((bf16[2,256,256]{1,2,0:T(8,128)(2,1)S(1)}, bf16[2,256,256]{1,2,0:T(8,128)(2,1)S(1)}, u32[]{:S(2)}, u32[]{:S(2)}) %collective-permute-start.3) | collective-permute-done | bytes 262176 | tf_op jit(solution)/shard_map/ppermute | solution.py:15
  233.2 2.1 copy.161
  236.9 59.6 %reduce-scatter.2.cloned.1.call-done = f32[2,256,512]{2,1,0:T(8,128)} async-done(((f32[2,256,2048]{2,1,0:T(8,128)}), f32[2,256,512]{2,1,0:T(8,128)}) %reduce-scatter.2.cloned.1.call-update) | async-done | bytes 1048592 | tf_op jit(solution)/shard_map/reduce_scatter | solution.py:101
  296.5 2.2 fusion.35
  (56 shorter events, 21.0 us)
Async XLA Ops:
  6.5 42.2 %all-gather.3.cloned.1.call-start = ((), (), s32[]{:S(2)}) async-start(), calls=%async_computation.2 | async-start | bytes 4718592 | tf_op jit(solution)/shard_map/all_gather | solution.py:64
  7.3 289.2 %reduce-scatter.2.cloned.1.call-start = ((), (), s32[]{:S(2)}) async-start(), calls=%async_computation.1 | async-start | bytes 5242880 | tf_op jit(solution)/shard_map/reduce_scatter | solution.py:101
  7.3 5.7 %copy-start.7 = (s32[1,14]{1,0:T(1,128)S(1)}, s32[1,14]{1,0:T(1,128)}, u32[]{:S(2)}) copy-start(s32[1,14]{1,0:T(1,128)} %param.13) | copy-start | bytes 172
  55.3 4.1 %copy-start.1 = (bf16[1,1,14,2,128,512]{5,4,2,3,1,0:T(8,128)(2,1)S(1)}, bf16[1,1,14,2,128,512]{5,4,2,3,1,0:T(8,128)(2,1)}, u32[]{:S(2)}) copy-start(bf16[1,1,14,2,128,512]{5,4,2,3,1,0:T(8,128)(2,1)} %copy.174) | copy-start | bytes 11010052
  66.6 42.5 %collective-permute-start = (bf16[14,2,256,128]{2,3,0,1:T(8,128)(2,1)}, bf16[14,2,256,128]{2,3,0,1:T(8,128)(2,1)}, u32[]{:S(2)}, u32[]{:S(2)}) collective-permute-start(bf16[14,2,256,128]{2,3,0,1:T(8,128)(2,1)} %pad_maximum_fusion.3), channel_id=1, source_target_pairs={{0,1},{1,0},{2,3},{3,2},{4,5},{5,4},{6,7},{7,6},{8,9},{9,8},{10,11... | collective-permute-start | bytes 5505032 | tf_op jit(solution)/shard_map/ppermute | solution.py:21
  114.5 81.9 %collective-permute-start.1 = (bf16[14,2,256,128]{2,3,0,1:T(8,128)(2,1)}, bf16[14,2,256,128]{2,3,0,1:T(8,128)(2,1)}, u32[]{:S(2)}, u32[]{:S(2)}) collective-permute-start(bf16[14,2,256,128]{2,3,0,1:T(8,128)(2,1)} %pad_maximum_fusion.4), channel_id=1, source_target_pairs={{0,2},{1,3},{2,0},{3,1},{4,6},{5,7},{6,4},{7,5},{8,10},{9,11},{10,... | collective-permute-start | bytes 5505032 | tf_op jit(solution)/shard_map/ppermute | solution.py:21
  211.3 1.0 copy-start.5
  212.3 6.3 %copy-start.6 = (s32[2,3]{1,0:T(2,128)S(1)}, s32[2,3]{1,0:T(2,128)}, u32[]{:S(2)}) copy-start(s32[2,3]{1,0:T(2,128)} %param.11) | copy-start | bytes 76
  212.6 18.4 %copy-start = (bf16[2,3,2,256,256]{4,3,2,1,0:T(8,128)(2,1)S(1)}, bf16[2,3,2,256,256]{4,3,2,1,0:T(8,128)(2,1)}, u32[]{:S(2)}) copy-start(bf16[2,3,2,256,256]{4,3,2,1,0:T(8,128)(2,1)} %param.10) | copy-start | bytes 4718596
  212.6 17.8 %collective-permute-start.3 = (bf16[2,256,256]{1,2,0:T(8,128)(2,1)S(1)}, bf16[2,256,256]{1,2,0:T(8,128)(2,1)S(1)}, u32[]{:S(2)}, u32[]{:S(2)}) collective-permute-start(bf16[2,256,256]{1,2,0:T(8,128)(2,1)S(1)} %get-tuple-element.20), channel_id=1, source_target_pairs={{1,0},{2,1},{3,2},{4,3},{5,4},{6,5},{7,6},{8,7},{9,8},{10,9},{11,1... | collective-permute-start | bytes 786440 | tf_op jit(solution)/shard_map/ppermute | solution.py:15
  214.0 16.8 %collective-permute-start.2 = (bf16[2,256,256]{1,2,0:T(8,128)(2,1)S(1)}, bf16[2,256,256]{1,2,0:T(8,128)(2,1)S(1)}, u32[]{:S(2)}, u32[]{:S(2)}) collective-permute-start(bf16[2,256,256]{1,2,0:T(8,128)(2,1)S(1)} %get-tuple-element.21), channel_id=1, source_target_pairs={{0,1},{1,2},{2,3},{3,4},{4,5},{5,6},{6,7},{7,8},{8,9},{9,10},{10,1... | collective-permute-start | bytes 786440 | tf_op jit(solution)/shard_map/ppermute | solution.py:12
  231.0 1.0 copy-start.2
  232.2 3.3 %copy-start.3 = (bf16[1,256,512]{1,2,0:T(8,128)(2,1)S(1)}, bf16[1,256,512]{1,2,0:T(8,128)(2,1)}, u32[]{:S(2)}) copy-start(bf16[1,256,512]{1,2,0:T(8,128)(2,1)} %copy-done.2) | copy-start | bytes 786436
  236.5 60.0 %copy-start.4 = (f32[1,256,512]{2,1,0:T(8,128)S(1)}, f32[1,256,512]{2,1,0:T(8,128)}, u32[]{:S(2)}) copy-start(f32[1,256,512]{2,1,0:T(8,128)} %copy.161) | copy-start | bytes 1572868
Sparse Core Ops, SparseCore 0:
  9.2 39.4 all-gather.2
  211.4 85.0 reduce-scatter.1
where the time goes:
time: 307 us; the launch traced here: 306 us
  waiting for transfers between devices  218 us (71%)
  local copies, waits for them, and re-layouts  25.3 us (8%)
  matrix products  22.3 us (7%)
  other arithmetic  16.6 us (5%)
  between operations  13.8 us (4%)
  starting transfers between devices  9.92 us (3%)
    ppermute x2, waiting for transfers between devices, partner_2(): lax.ppermute(value, axis, [(i, i ^ 1 << stride) for i in range(lax.axis_s...  110 us
    reduce_scatter x1, waiting for transfers between devices, on_device(): far = lax.psum_scatter(terms, 'mem', scatter_dimension=2, tiled=True)  59.6 us
    all_gather x1, waiting for transfers between devices, on_device(): arrived = lax.all_gather(incident[None], 'grp', axis=0, tiled=True)  35.6 us
    dot_general x28, matrix products, mult(): return jnp.einsum(form, left, right, preferred_element_type=jnp.float32)  22.3 us
    unnamed x21, local copies, waits for them, and re-layouts  16.4 us
    ppermute x1, waiting for transfers between devices, with_halo(): lax.ppermute(lax.slice_in_dim(block, 0, width, axis=dim), axis, backward)  11.6 us
    gather x1, local copies, waits for them, and re-layouts, on_device(): chosen = jnp.take(arrived, sources, axis=0)  6.64 us
  transfers between devices with their start and end apart: 6, of which 6 were waited for; matrix products, arithmetic and copies ran while one was open for 7% of the time, Pallas kernels for 0%

commit v1 on v0

--- a/solution.py
+++ b/solution.py
@@ -3,18 +3,7 @@
 from jax import lax
 from jax.sharding import PartitionSpec as P
 
-
-def with_halo(block, sides, width):
-    for axis, dim in sides:
-        count = lax.axis_size(axis)
-        forward = [(i, i + 1) for i in range(count - 1)]
-        backward = [(target, source) for source, target in forward]
-        low = lax.ppermute(
-            lax.slice_in_dim(block, block.shape[dim] - width, None, axis=dim), axis, forward
-        )
-        high = lax.ppermute(lax.slice_in_dim(block, 0, width, axis=dim), axis, backward)
-        block = jnp.concatenate([low, block, high], axis=dim)
-    return block
+PARTS = 2
 
 
 def partner_2(value, axis, stride):
@@ -60,10 +49,21 @@
     rank_size = basis_in.shape[4]
     group = lax.axis_index("grp")
     member = lax.axis_index("mem")
+    bits = (member % 2, member // 2 % 2)
+    count = lax.axis_size("grp") * lax.axis_size("mem")
+    forward = [(i, i + 1) for i in range(count - 1)]
+    backward = [(b, a) for a, b in forward]
+    low = lax.ppermute(incident[:, :, row_count - leaf_size :], ("grp", "mem"), forward)
+    high = lax.ppermute(incident[:, :, :leaf_size], ("grp", "mem"), backward)
+    padded = jnp.concatenate([low, incident, high], axis=2)
     sources = lax.dynamic_slice_in_dim(far_source, group, 1, 0)[0]
     arrived = lax.all_gather(incident[None], "grp", axis=0, tiled=True)
-    chosen = jnp.take(arrived, sources, axis=0)
-    padded = with_halo(incident, ((("grp", "mem"), 2),), leaf_size)
+    chosen = jnp.stack(
+        [
+            lax.dynamic_index_in_dim(arrived, sources[f], 0, keepdims=False)
+            for f in range(far_source.shape[1])
+        ]
+    )
     near_real = jnp.zeros((nrhs_count, leaf_count, leaf_size), jnp.float32)
     near_imag = jnp.zeros((nrhs_count, leaf_count, leaf_size), jnp.float32)
     for offset in range(3):
@@ -85,20 +85,31 @@
     )
     keep = (jnp.arange(rank_size)[None, :] < far_rank[0][:, None]).astype(jnp.float32)[:, None, :]
     factor = basis_in[0, 0]
-    first, second = complex_apply(
-        factor[:, 0], factor[:, 1], chosen[:, 0], chosen[:, 1], "fkr,fnr->fnk"
-    )
-    level = jnp.stack([first * keep, second * keep], 1).astype(jnp.bfloat16)
-    partner = partner_2(level, "mem", 0)
-    level = mix_section(level, partner, member % 2, section_one[0, 0], keep)
-    partner = partner_2(level, "mem", 1)
-    level = mix_section(level, partner, member // 2 % 2, section_two[0, 0], keep)
     outward = basis_out[0, 0]
-    first, second = complex_apply(
-        outward[:, 0], outward[:, 1], level[:, 0], level[:, 1], "frk,fnk->nr"
-    )
-    terms = jnp.stack([first, second], 0)
-    far = lax.psum_scatter(terms, "mem", scatter_dimension=2, tiled=True)
+    width = nrhs_count // PARTS
+    pieces = []
+    for part in range(PARTS):
+        source = chosen[:, :, part * width : (part + 1) * width]
+        first, second = complex_apply(
+            factor[:, 0], factor[:, 1], source[:, 0], source[:, 1], "fkr,fnr->fnk"
+        )
+        level = jnp.stack([first * keep, second * keep], 1).astype(jnp.bfloat16)
+        partner = partner_2(level, "mem", 0)
+        level = mix_section(level, partner, bits[0], section_one[0, 0], keep)
+        partner = partner_2(level, "mem", 1)
+        level = mix_section(level, partner, bits[1], section_two[0, 0], keep)
+        first, second = complex_apply(
+            outward[:, 0], outward[:, 1], level[:, 0], level[:, 1], "frk,fnk->nr"
+        )
+        terms = jnp.stack([first, second], 0).reshape(2, width, 2, 2, row_count)
+        sent = lax.dynamic_index_in_dim(terms, 1 - bits[0], 3, keepdims=False)
+        held = lax.dynamic_index_in_dim(terms, bits[0], 3, keepdims=False)
+        held = held + partner_2(sent.astype(jnp.bfloat16), "mem", 0).astype(jnp.float32)
+        sent = lax.dynamic_index_in_dim(held, 1 - bits[1], 2, keepdims=False)
+        held = lax.dynamic_index_in_dim(held, bits[1], 2, keepdims=False)
+        held = held + partner_2(sent.astype(jnp.bfloat16), "mem", 1).astype(jnp.float32)
+        pieces.append(held)
+    far = jnp.concatenate(pieces, 1)
     return (far + near).astype(jnp.bfloat16)
 
 

time: 307 us -> 317 us (1.033)
  waiting for transfers between devices: 218 us -> 133 us
  matrix products: 22.3 us -> 61.9 us
  local copies, waits for them, and re-layouts: 25.3 us -> 52.8 us
  between operations: 13.8 us -> 40.6 us
  starting transfers between devices: 9.92 us -> 20.7 us
  other arithmetic: 16.6 us -> 6.57 us
    reduce_scatter x1 -> x0, waiting for transfers between devices: 59.6 us -> none  [on_device(): far = lax.psum_scatter(terms, 'mem', scatter_dimension=2, tiled=True)]
    dot_general x28 -> x44, matrix products: 22.3 us -> 61.9 us  [mult(): return jnp.einsum(form, left, right, preferred_element_type=jnp.float32)]
    all_gather x1, waiting for transfers between devices: 35.6 us -> 0.01 us  [on_device(): arrived = lax.all_gather(incident[None], 'grp', axis=0, tiled=True)]
    ppermute x2 -> x8, waiting for transfers between devices: 110 us -> 132 us  [partner_2(): lax.ppermute(value, axis, [(i, i ^ 1 << stride) for i in range(lax.axis_s...]
    unnamed x21 -> x82, local copies, waits for them, and re-layouts: 16.4 us -> 36.7 us
    ppermute x2, waiting for transfers between devices: 12 us -> 0.01 us  [the longest x1 0.01 us: on_device(): high = lax.ppermute(incident[:, :, :leaf_size], ('grp', 'mem'), backward)]
    another operation x0 -> x7, local copies, waits for them, and re-layouts: none -> 11.1 us  [the longest x6 11.1 us: on_device(): terms = jnp.stack([first, second], 0).reshape(2, width, 2, 2, row_count)]
    ppermute x2 -> x8, starting transfers between devices: 3.89 us -> 13.9 us  [partner_2(): lax.ppermute(value, axis, [(i, i ^ 1 << stride) for i in range(lax.axis_s...]
  transfers between devices with their start and end apart: 6 -> 11, of which waited for: 6 -> 6; matrix products, arithmetic and copies ran while one was open for 7% -> 22% of each run, Pallas kernels for 0% -> 0%
where the time goes in v1:
time: 317 us; the launch traced here: 316 us
  waiting for transfers between devices  133 us (42%)
  matrix products  61.9 us (20%)
  local copies, waits for them, and re-layouts  52.8 us (17%)
  between operations  40.6 us (13%)
  starting transfers between devices  20.7 us (7%)
  other arithmetic  6.57 us (2%)
    ppermute x8, waiting for transfers between devices, partner_2(): lax.ppermute(value, axis, [(i, i ^ 1 << stride) for i in range(lax.axis_s...  132 us
    dot_general x44, matrix products, mult(): return jnp.einsum(form, left, right, preferred_element_type=jnp.float32)  61.9 us
    unnamed x82, local copies, waits for them, and re-layouts  36.7 us
    ppermute x8, starting transfers between devices, partner_2(): lax.ppermute(value, axis, [(i, i ^ 1 << stride) for i in range(lax.axis_s...  13.9 us
    another operation x6, local copies, waits for them, and re-layouts, on_device(): terms = jnp.stack([first, second], 0).reshape(2, width, 2, 2, row_count)  11.1 us
  transfers between devices with their start and end apart: 11, of which 6 were waited for; matrix products, arithmetic and copies ran while one was open for 22% of the time, Pallas kernels for 0%

profile of v1, /device:TPU:0, one launch (start us, length us, event | category | flops | bytes accessed | tf_op | source)
XLA Modules:
  0.0 315.5 jit_solution(9861995269787135370)
XLA Ops:
  9.9 5.6 %collective-permute-start.8 = (bf16[2,256,256]{1,2,0:T(8,128)(2,1)S(1)}, bf16[2,256,256]{1,2,0:T(8,128)(2,1)S(1)}, u32[]{:S(2)}, u32[]{:S(2)}) collective-permute-start(bf16[2,256,256]{1,2,0:T(8,128)(2,1)S(1)} %get-tuple-element.25), channel_id=1, source_target_pairs={{0,1},{1,2},{2,3},{3,4},{4,5},{5,6},{6,7},{7,8},{8,9},{9,10},{10,1... | collective-permute-start | bytes 786440 | tf_op jit(solution)/shard_map/ppermute | solution.py:56
  38.4 2.1 copy.291
  40.5 13.9 %copy.290 = bf16[1,1,14,2,2048,128]{5,4,2,3,1,0:T(8,128)(2,1)} copy(bf16[1,1,14,2,2048,128]{5,4,3,2,1,0:T(8,128)(2,1)} %param.17) | data formatting | bytes 29360128 | tf_op args[8]
  79.4 2.0 collective-permute-start
  84.4 17.7 %collective-permute-done = bf16[14,2,128,128]{2,3,0,1:T(8,128)(2,1)S(1)} collective-permute-done((bf16[14,2,128,128]{2,3,0,1:T(8,128)(2,1)S(1)}, bf16[14,2,128,128]{2,3,0,1:T(8,128)(2,1)S(1)}, u32[]{:S(2)}, u32[]{:S(2)}) %collective-permute-start) | collective-permute-done | bytes 917536 | tf_op jit(solution)/shard_map/ppermute | solution.py:10
  103.0 18.2 %collective-permute-done.4 = bf16[14,2,128,128]{2,3,0,1:T(8,128)(2,1)S(1)} collective-permute-done((bf16[14,2,128,128]{2,3,0,1:T(8,128)(2,1)S(1)}, bf16[14,2,128,128]{2,3,0,1:T(8,128)(2,1)S(1)}, u32[]{:S(2)}, u32[]{:S(2)}) %collective-permute-start.4) | collective-permute-done | bytes 917536 | tf_op jit(solution)/shard_map/ppermute | solution.py:10
  123.1 5.2 %collective-permute-start.1 = (bf16[14,2,128,128]{2,3,0,1:T(8,128)(2,1)S(1)}, bf16[14,2,128,128]{2,3,0,1:T(8,128)(2,1)S(1)}, u32[]{:S(2)}, u32[]{:S(2)}) collective-permute-start(bf16[14,2,128,128]{2,3,0,1:T(8,128)(2,1)S(1)} %pad_maximum_fusion.5), channel_id=1, source_target_pairs={{0,2},{1,3},{2,0},{3,1},{4,6},{5,7},{6,4},{7,5},{8,10},{9,11},{10,... | collective-permute-start | bytes 2752520 | tf_op jit(solution)/shard_map/ppermute | solution.py:10
  131.2 57.5 %collective-permute-done.1 = bf16[14,2,128,128]{2,3,0,1:T(8,128)(2,1)S(1)} collective-permute-done((bf16[14,2,128,128]{2,3,0,1:T(8,128)(2,1)S(1)}, bf16[14,2,128,128]{2,3,0,1:T(8,128)(2,1)S(1)}, u32[]{:S(2)}, u32[]{:S(2)}) %collective-permute-start.1) | collective-permute-done | bytes 917536 | tf_op jit(solution)/shard_map/ppermute | solution.py:10
  189.7 18.2 %collective-permute-done.5 = bf16[14,2,128,128]{2,3,0,1:T(8,128)(2,1)S(1)} collective-permute-done((bf16[14,2,128,128]{2,3,0,1:T(8,128)(2,1)S(1)}, bf16[14,2,128,128]{2,3,0,1:T(8,128)(2,1)S(1)}, u32[]{:S(2)}, u32[]{:S(2)}) %collective-permute-start.5) | collective-permute-done | bytes 917536 | tf_op jit(solution)/shard_map/ppermute | solution.py:10
  213.8 2.5 fusion.9
  216.3 3.5 %fusion.8 = f32[128,2048]{1,0:T(8,128)} fusion(bf16[14,128,128]{1,2,0:T(8,128)(2,1)S(1)} %fusion.45, bf16[14,2,2048,128]{3,2,0,1:T(8,128)(2,1)S(1)} %bitcast.374), kind=kOutput, calls=%fused_computation.12 | convolution fusion | flops 939524096 | bytes 8847360 | tf_op jit(solution)/shard_map/frk,fnk->nr/dot_general | solution.py:16
  219.8 3.5 %fusion.18 = f32[128,2048]{1,0:T(8,128)} fusion(f32[128,2048]{1,0:T(8,128)S(1)} %fusion.9, bf16[14,128,128]{1,2,0:T(8,128)(2,1)S(1)} %fusion.45, bf16[14,2,2048,128]{3,2,0,1:T(8,128)(2,1)S(1)} %bitcast.375), kind=kOutput, calls=%fused_computation.22 | convolution fusion | flops 939786240 | bytes 9895936 | tf_op jit(solution)/shard_map/frk,fnk->nr/dot_general | solution.py:16
  223.3 2.2 stack.106
  225.5 6.9 %fusion.19 = f32[128,2048]{1,0:T(8,128)} fusion(f32[128,2048]{1,0:T(8,128)} %fusion.8, bf16[14,128,128]{1,2,0:T(8,128)(2,1)S(1)} %copy-done.26, bf16[14,2,2048,128]{3,2,0,1:T(8,128)(2,1)} %bitcast.366), kind=kOutput, calls=%fused_computation.23 | convolution fusion | flops 939786240 | bytes 9895936 | tf_op jit(solution)/shard_map/frk,fnk->nr/dot_general | solution.py:16
  232.4 3.1 stack.105
  239.5 5.6 %fusion.10 = f32[128,2048]{1,0:T(8,128)S(1)} fusion(bf16[14,128,128]{1,2,0:T(8,128)(2,1)S(1)} %copy-done.21, bf16[14,2,2048,128]{3,2,0,1:T(8,128)(2,1)} %bitcast.367), kind=kOutput, calls=%fused_computation.14 | convolution fusion | flops 939524096 | bytes 8847360 | tf_op jit(solution)/shard_map/frk,fnk->nr/dot_general | solution.py:16
  245.2 6.9 %fusion.11 = f32[128,2048]{1,0:T(8,128)} fusion(bf16[14,128,128]{1,2,0:T(8,128)(2,1)S(1)} %copy-done.24, bf16[14,2,2048,128]{3,2,0,1:T(8,128)(2,1)} %bitcast.368), kind=kOutput, calls=%fused_computation.15 | convolution fusion | flops 939524096 | bytes 8847360 | tf_op jit(solution)/shard_map/frk,fnk->nr/dot_general | solution.py:16
  252.1 6.6 %fusion.17 = f32[128,2048]{1,0:T(8,128)} fusion(f32[128,2048]{1,0:T(8,128)S(1)} %fusion.10, bf16[14,128,128]{1,2,0:T(8,128)(2,1)S(1)} %copy-done.24, bf16[14,2,2048,128]{3,2,0,1:T(8,128)(2,1)} %bitcast.369), kind=kOutput, calls=%fused_computation.21 | convolution fusion | flops 939786240 | bytes 9895936 | tf_op jit(solution)/shard_map/frk,fnk->nr/dot_general | solution.py:16
  258.7 2.1 stack.114
  260.8 7.0 %fusion.16 = f32[128,2048]{1,0:T(8,128)} fusion(f32[128,2048]{1,0:T(8,128)} %fusion.11, bf16[14,128,128]{1,2,0:T(8,128)(2,1)} %fusion.47, bf16[14,2,2048,128]{3,2,0,1:T(8,128)(2,1)} %bitcast.370), kind=kOutput, calls=%fused_computation.20 | convolution fusion | flops 939786240 | bytes 9895936 | tf_op jit(solution)/shard_map/frk,fnk->nr/dot_general | solution.py:16
  267.8 3.1 stack.115
  276.2 3.0 collective-permute-start.3
  279.2 12.6 %collective-permute-done.6 = bf16[2,128,2,512]{3,1,0,2:T(8,128)(2,1)S(1)} collective-permute-done((bf16[2,128,2,512]{3,1,0,2:T(8,128)(2,1)S(1)}, bf16[2,128,2,512]{3,1,0,2:T(8,128)(2,1)S(1)}, u32[]{:S(2)}, u32[]{:S(2)}) %collective-permute-start.6) | collective-permute-done | bytes 524320 | tf_op jit(solution)/shard_map/ppermute | solution.py:10
  298.7 7.9 %collective-permute-done.7 = bf16[2,128,512]{2,1,0:T(8,128)(2,1)} collective-permute-done((bf16[2,128,512]{2,1,0:T(8,128)(2,1)}, bf16[2,128,512]{2,1,0:T(8,128)(2,1)}, u32[]{:S(2)}, u32[]{:S(2)}) %collective-permute-start.7) | collective-permute-done | bytes 262176 | tf_op jit(solution)/shard_map/ppermute | solution.py:10
  (158 shorter events, 57.9 us)
Async XLA Ops:
  6.5 8.9 %copy-start = (s32[8,14]{1,0:T(8,128)S(1)}, s32[8,14]{1,0:T(8,128)}, u32[]{:S(2)}) copy-start(s32[8,14]{1,0:T(8,128)} %param.12) | copy-start | bytes 1348
  6.5 9.6 %copy-start.22 = (s32[2,3]{1,0:T(2,128)S(1)}, s32[2,3]{1,0:T(2,128)}, u32[]{:S(2)}) copy-start(s32[2,3]{1,0:T(2,128)} %param.11) | copy-start | bytes 76
  6.5 27.5 %copy-start.19 = (bf16[1,1,14,2,128,256]{5,4,3,2,1,0:T(8,128)(2,1)S(1)}, bf16[1,1,14,2,128,256]{5,4,3,2,1,0:T(8,128)(2,1)}, u32[]{:S(2)}) copy-start(bf16[1,1,14,2,128,256]{5,4,3,2,1,0:T(8,128)(2,1)} %param.15) | copy-start | bytes 5505028
  6.5 61.8 %all-gather.3.cloned.1.call-start = ((), (), s32[]{:S(2)}) async-start(), calls=%async_computation | async-start | bytes 4718592 | tf_op jit(solution)/shard_map/all_gather | solution.py:60
  8.6 54.8 %collective-permute-start.9 = (bf16[2,256,256]{1,2,0:T(8,128)(2,1)S(1)}, bf16[2,256,256]{1,2,0:T(8,128)(2,1)S(1)}, u32[]{:S(2)}, u32[]{:S(2)}) collective-permute-start(bf16[2,256,256]{1,2,0:T(8,128)(2,1)S(1)} %get-tuple-element.24), channel_id=1, source_target_pairs={{1,0},{2,1},{3,2},{4,3},{5,4},{6,5},{7,6},{8,7},{9,8},{10,9},{11,1... | collective-permute-start | bytes 786440 | tf_op jit(solution)/shard_map/ppermute | solution.py:57
  9.9 53.5 %collective-permute-start.8 = (bf16[2,256,256]{1,2,0:T(8,128)(2,1)S(1)}, bf16[2,256,256]{1,2,0:T(8,128)(2,1)S(1)}, u32[]{:S(2)}, u32[]{:S(2)}) collective-permute-start(bf16[2,256,256]{1,2,0:T(8,128)(2,1)S(1)} %get-tuple-element.25), channel_id=1, source_target_pairs={{0,1},{1,2},{2,3},{3,4},{4,5},{5,6},{6,7},{7,8},{8,9},{9,10},{10,1... | collective-permute-start | bytes 786440 | tf_op jit(solution)/shard_map/ppermute | solution.py:56
  40.5 22.7 %copy-start.23 = (s32[1,14]{1,0:T(1,128)S(1)}, s32[1,14]{1,0:T(1,128)}, u32[]{:S(2)}) copy-start(s32[1,14]{1,0:T(1,128)} %param.13) | copy-start | bytes 172
  68.4 4.7 %copy-start.3 = (bf16[16,256,512]{2,1,0:T(8,128)(2,1)S(1)}, bf16[16,256,512]{2,1,0:T(8,128)(2,1)}, u32[]{:S(2)}) copy-start(bf16[16,256,512]{2,1,0:T(8,128)(2,1)} %all-gather.3.cloned.1.call-done) | copy-start | bytes 12582916
  79.4 22.7 %collective-permute-start = (bf16[14,2,128,128]{2,3,0,1:T(8,128)(2,1)S(1)}, bf16[14,2,128,128]{2,3,0,1:T(8,128)(2,1)S(1)}, u32[]{:S(2)}, u32[]{:S(2)}) collective-permute-start(bf16[14,2,128,128]{2,3,0,1:T(8,128)(2,1)S(1)} %pad_maximum_fusion.4), channel_id=1, source_target_pairs={{0,1},{1,0},{2,3},{3,2},{4,5},{5,4},{6,7},{7,6},{8,9},{9,8},{10,11... | collective-permute-start | bytes 2752520 | tf_op jit(solution)/shard_map/ppermute | solution.py:10
  82.8 38.4 %collective-permute-start.4 = (bf16[14,2,128,128]{2,3,0,1:T(8,128)(2,1)S(1)}, bf16[14,2,128,128]{2,3,0,1:T(8,128)(2,1)S(1)}, u32[]{:S(2)}, u32[]{:S(2)}) collective-permute-start(bf16[14,2,128,128]{2,3,0,1:T(8,128)(2,1)S(1)} %pad_maximum_fusion.6), channel_id=1, source_target_pairs={{0,1},{1,0},{2,3},{3,2},{4,5},{5,4},{6,7},{7,6},{8,9},{9,8},{10,11... | collective-permute-start | bytes 2752520 | tf_op jit(solution)/shard_map/ppermute | solution.py:10
  84.4 17.8 %copy-start.2 = (bf16[1,1,14,2,128,256]{5,4,2,3,1,0:T(8,128)(2,1)S(1)}, bf16[1,1,14,2,128,256]{5,4,2,3,1,0:T(8,128)(2,1)}, u32[]{:S(2)}) copy-start(bf16[1,1,14,2,128,256]{5,4,2,3,1,0:T(8,128)(2,1)} %copy.293) | copy-start | bytes 5505028
  123.1 65.6 %collective-permute-start.1 = (bf16[14,2,128,128]{2,3,0,1:T(8,128)(2,1)S(1)}, bf16[14,2,128,128]{2,3,0,1:T(8,128)(2,1)S(1)}, u32[]{:S(2)}, u32[]{:S(2)}) collective-permute-start(bf16[14,2,128,128]{2,3,0,1:T(8,128)(2,1)S(1)} %pad_maximum_fusion.5), channel_id=1, source_target_pairs={{0,2},{1,3},{2,0},{3,1},{4,6},{5,7},{6,4},{7,5},{8,10},{9,11},{10,... | collective-permute-start | bytes 2752520 | tf_op jit(solution)/shard_map/ppermute | solution.py:10
  129.2 78.7 %collective-permute-start.5 = (bf16[14,2,128,128]{2,3,0,1:T(8,128)(2,1)S(1)}, bf16[14,2,128,128]{2,3,0,1:T(8,128)(2,1)S(1)}, u32[]{:S(2)}, u32[]{:S(2)}) collective-permute-start(bf16[14,2,128,128]{2,3,0,1:T(8,128)(2,1)S(1)} %pad_maximum_fusion.7), channel_id=1, source_target_pairs={{0,2},{1,3},{2,0},{3,1},{4,6},{5,7},{6,4},{7,5},{8,10},{9,11},{10,... | collective-permute-start | bytes 2752520 | tf_op jit(solution)/shard_map/ppermute | solution.py:10
  207.9 4.5 %slice-start = ((s8[14680064]{0:T(1024)(128)(4,1)}), s8[4194304]{0:T(1024)(128)(4,1)S(1)}, s32[]{:S(2)}) async-start(s8[14680064]{0:T(1024)(128)(4,1)} %bitcast.371), calls=%async_computation.1 | async-start | bytes 8388608
  208.8 4.4 %slice-start.2 = ((s8[14680064]{0:T(1024)(128)(4,1)}), s8[4194304]{0:T(1024)(128)(4,1)S(1)}, s32[]{:S(2)}) async-start(s8[14680064]{0:T(1024)(128)(4,1)} %bitcast.371), calls=%async_computation.3 | async-start | bytes 8388608
  238.7 6.5 %copy-start.24 = (bf16[14,128,128]{1,2,0:T(8,128)(2,1)S(1)}, bf16[14,128,128]{1,2,0:T(8,128)(2,1)}, u32[]{:S(2)}) copy-start(bf16[14,128,128]{1,2,0:T(8,128)(2,1)} %multiply_convert_fusion) | copy-start | bytes 1376260
  238.8 35.4 %collective-permute-start.2 = (bf16[2,128,2,512]{3,1,0,2:T(8,128)(2,1)S(1)}, bf16[2,128,2,512]{3,1,0,2:T(8,128)(2,1)}, u32[]{:S(2)}, u32[]{:S(2)}) collective-permute-start(bf16[2,128,2,512]{3,1,0,2:T(8,128)(2,1)S(1)} %fusion.91), channel_id=1, source_target_pairs={{0,1},{1,0},{2,3},{3,2},{4,5},{5,4},{6,7},{7,6},{8,9},{9,8},{10,11... | collective-permute-start | bytes 1572872 | tf_op jit(solution)/shard_map/ppermute | solution.py:10
  272.5 19.2 %collective-permute-start.6 = (bf16[2,128,2,512]{3,1,0,2:T(8,128)(2,1)S(1)}, bf16[2,128,2,512]{3,1,0,2:T(8,128)(2,1)S(1)}, u32[]{:S(2)}, u32[]{:S(2)}) collective-permute-start(bf16[2,128,2,512]{3,1,0,2:T(8,128)(2,1)S(1)} %fusion.92), channel_id=1, source_target_pairs={{0,1},{1,0},{2,3},{3,2},{4,5},{5,4},{6,7},{7,6},{8,9},{9,8},{10,11... | collective-permute-start | bytes 1572872 | tf_op jit(solution)/shard_map/ppermute | solution.py:10
  275.4 18.6 %copy-start.14 = (bf16[1,256,512]{1,2,0:T(8,128)(2,1)S(1)}, bf16[1,256,512]{1,2,0:T(8,128)(2,1)}, u32[]{:S(2)}) copy-start(bf16[1,256,512]{1,2,0:T(8,128)(2,1)} %get-tuple-element.17) | copy-start | bytes 786436
  275.4 18.6 %copy-start.17 = (f32[2,256,256]{1,2,0:T(8,128)S(1)}, f32[2,256,256]{1,2,0:T(8,128)}, u32[]{:S(2)}) copy-start(f32[2,256,256]{1,2,0:T(8,128)} %fusion.56) | copy-start | bytes 1572868
  276.2 21.5 %collective-permute-start.3 = (bf16[2,128,512]{2,1,0:T(8,128)(2,1)}, bf16[2,128,512]{2,1,0:T(8,128)(2,1)}, u32[]{:S(2)}, u32[]{:S(2)}) collective-permute-start(bf16[2,128,512]{2,1,0:T(8,128)(2,1)} %fusion.93), channel_id=1, source_target_pairs={{0,2},{1,3},{2,0},{3,1},{4,6},{5,7},{6,4},{7,5},{8,10},{9,11},{10,... | collective-permute-start | bytes 786440 | tf_op jit(solution)/shard_map/ppermute | solution.py:10
  292.8 13.9 %collective-permute-start.7 = (bf16[2,128,512]{2,1,0:T(8,128)(2,1)}, bf16[2,128,512]{2,1,0:T(8,128)(2,1)}, u32[]{:S(2)}, u32[]{:S(2)}) collective-permute-start(bf16[2,128,512]{2,1,0:T(8,128)(2,1)} %fusion.94), channel_id=1, source_target_pairs={{0,2},{1,3},{2,0},{3,1},{4,6},{5,7},{6,4},{7,5},{8,10},{9,11},{10,... | collective-permute-start | bytes 786440 | tf_op jit(solution)/shard_map/ppermute | solution.py:10
  295.1 11.6 %copy-start.12 = (f32[2,128,2,512]{3,1,0,2:T(8,128)S(1)}, f32[2,128,2,512]{3,1,0,2:T(8,128)}, u32[]{:S(2)}) copy-start(f32[2,128,2,512]{3,1,0,2:T(8,128)} %copy-done.11) | copy-start | bytes 3145732
  297.7 11.0 %copy-start.1 = (s32[8,14]{1,0:T(8,128)S(1)}, s32[8,14]{1,0:T(8,128)}, u32[]{:S(2)}) copy-start(s32[8,14]{1,0:T(8,128)} %param.12) | copy-start | bytes 1348
  (18 other events, 38.1 us)
Sparse Core Ops, SparseCore 0:
  9.3 40.4 all-gather.2

commit v2 on v0

v2 whole, which is shorter than its diff:
```python
import functools

import jax
import jax.numpy as jnp
from jax import lax
from jax.experimental import pallas as pl
from jax.experimental.pallas import tpu as pltpu
from jax.sharding import PartitionSpec as P

MESH = pl.DeviceIdType.MESH
PARTS = 4
CUTS = 2


def dot_nt(left, right):
    return lax.dot_general(
        left, right, (((1,), (1,)), ((), ())), preferred_element_type=jnp.float32
    )


def kernel(
    groups,
    members,
    incident,
    near_blocks,
    near_mask,
    far_source,
    far_rank,
    basis_in,
    section_one,
    section_two,
    basis_out,
    out,
    arrived,
    halo,
    w_near,
    w_in,
    w_one,
    w_two,
    w_out,
    level0,
    level0p,
    level1,
    level1p,
    level2,
    near,
    held,
    send1,
    recv1,
    send2,
    recv2,
    load_sem,
    gather_send,
    gather_recv,
    halo_send,
    halo_recv,
    l0_send,
    l0_recv,
    l1_send,
    l1_recv,
    r1_send,
    r1_recv,
    r2_send,
    r2_recv,
):
    rhs, rows = incident.shape[1], incident.shape[2]
    leaves, leaf = near_blocks.shape[0], near_blocks.shape[3]
    far, rank = w_in.shape[0], w_in.shape[2]
    parts = level0.shape[0]
    width = rhs // parts
    cuts = l0_send.shape[0] // parts
    per = far // cuts
    units = parts * cuts
    tile = min(256, rows)
    tiles = rows // tile

    group = lax.axis_index("grp")
    member = lax.axis_index("mem")
    bit0 = lax.rem(member, 2)
    bit1 = lax.rem(member // 2, 2)
    across0 = {"mem": member + 1 - 2 * bit0}
    across1 = {"mem": member + 2 - 4 * bit1}
    count = groups * members
    flat = group * members + member
    after = lax.rem(flat + 1, count)
    before = lax.rem(flat + count - 1, count)
    after_id = {"grp": after // members, "mem": lax.rem(after, members)}
    before_id = {"grp": before // members, "mem": lax.rem(before, members)}
    bits = groups.bit_length() - 1
    group_bits = [lax.rem(group // (1 << b), 2) for b in range(bits)]

    def flipped(mask):
        value = group
        for b in range(bits):
            if mask >> b & 1:
                value = value + (1 - 2 * group_bits[b]) * (1 << b)
        return value

    own = pltpu.make_async_copy(incident, arrived.at[group], load_sem.at[0])
    own.start()
    loads = []
    for i, (source, target) in enumerate(
        (
            (basis_in.at[0, 0], w_in),
            (near_blocks, w_near),
            (section_one.at[0, 0], w_one),
            (section_two.at[0, 0], w_two),
            (basis_out.at[0, 0], w_out),
        )
    ):
        load = pltpu.make_async_copy(source, target, load_sem.at[i + 1])
        load.start()
        loads.append(load)
    load_in, load_near, load_one, load_two, load_out = loads

    barrier = pltpu.get_barrier_semaphore()
    greeted = [{"grp": flipped(1 << b)} for b in range(bits)]
    greeted += [across0, across1, after_id, before_id]
    for neighbour in greeted:
        pl.semaphore_signal(barrier, inc=1, device_id=neighbour, device_id_type=MESH)
    pl.semaphore_wait(barrier, len(greeted))

    started = []

    def send(source, target, send_sem, recv_sem, device):
        copy = pltpu.make_async_remote_copy(
            src_ref=source,
            dst_ref=target,
            send_sem=send_sem,
            recv_sem=recv_sem,
            device_id=device,
            device_id_type=MESH,
        )
        copy.start()
        started.append(copy)
        return copy

    halos = [
        send(
            incident.at[:, :, pl.ds(rows - leaf, leaf)],
            halo.at[0],
            halo_send.at[0],
            halo_recv.at[0],
            after_id,
        ),
        send(
            incident.at[:, :, pl.ds(0, leaf)],
            halo.at[1],
            halo_send.at[1],
            halo_recv.at[1],
            before_id,
        ),
    ]

    own.wait()
    outer = list(range(1, bits))
    orders = (outer, outer[::-1])
    number = [0, 0]

    def pass_on(half, mask, bit):
        slot = arrived.at[flipped(mask), half]
        j = number[half]
        number[half] += 1
        return send(
            slot, slot, gather_send.at[half, j], gather_recv.at[half, j], {"grp": flipped(1 << bit)}
        )

    masks = [[0], [0]]
    sideways = []
    pending = []
    for half in range(2):
        if outer:
            pending.append((half, [pass_on(half, 0, orders[half][0])]))
    for half in range(2):
        sideways.append(pass_on(half, 0, 0))
    for stage in range(len(outer)):
        later = []
        for half, copies in pending:
            for copy in copies:
                copy.wait_recv()
            fresh = [mask ^ 1 << orders[half][stage] for mask in masks[half]]
            masks[half] = masks[half] + fresh
            if stage + 1 < len(outer):
                later.append(
                    (half, [pass_on(half, mask, orders[half][stage + 1]) for mask in masks[half]])
                )
            for mask in fresh:
                sideways.append(pass_on(half, mask, 0))
        pending = later
    load_in.wait()
    for copy in sideways:
        copy.wait_recv()

    def combine(product):
        first = product[:width, :rank] - product[width:, rank:]
        second = product[width:, :rank] + product[:width, rank:]
        return first, second

    def kept(value, f):
        lanes = lax.broadcasted_iota(jnp.int32, value.shape, 1)
        return jnp.where(lanes < far_rank[0, f], value, 0.0)

    def stage_a(unit):
        part, cut = divmod(unit, cuts)

        def body(i, carry):
            f = cut * per + i
            x = arrived[far_source[group, f], :, part * width : (part + 1) * width, :]
            first, second = combine(
                dot_nt(x.reshape(2 * width, rows), w_in[f].reshape(2 * rank, rows))
            )
            level0[part, f, 0] = kept(first, f).astype(jnp.bfloat16)
            level0[part, f, 1] = kept(second, f).astype(jnp.bfloat16)
            return carry

        lax.fori_loop(0, per, body, 0)
        chunk = pl.ds(cut * per, per)
        return send(
            level0.at[part, chunk],
            level0p.at[part, chunk],
            l0_send.at[unit],
            l0_recv.at[unit],
            across0,
        )

    def mix(part, f, mine, theirs, weights, bit):
        x = jnp.concatenate(
            [mine[part, f].reshape(2 * width, rank), theirs[part, f].reshape(2 * width, rank)], 1
        )
        lower = pl.ds(pl.multiple_of(bit * rank, rank), rank)
        upper = pl.ds(pl.multiple_of((1 - bit) * rank, rank), rank)
        w = jnp.concatenate(
            [
                weights[f, :, :, lower].reshape(2 * rank, rank),
                weights[f, :, :, upper].reshape(2 * rank, rank),
            ],
            1,
        )
        first, second = combine(dot_nt(x, w))
        return kept(first, f).astype(jnp.bfloat16), kept(second, f).astype(jnp.bfloat16)

    def stage_b(unit):
        part, cut = divmod(unit, cuts)

        def body(i, carry):
            f = cut * per + i
            first, second = mix(part, f, level0, level0p, w_one, bit0)
            level1[part, f, 0] = first
            level1[part, f, 1] = second
            return carry

        lax.fori_loop(0, per, body, 0)
        chunk = pl.ds(cut * per, per)
        return send(
            level1.at[part, chunk],
            level1p.at[part, chunk],
            l1_send.at[unit],
            l1_recv.at[unit],
            across1,
        )

    def stage_d(unit):
        part, cut = divmod(unit, cuts)

        def body(i, carry):
            f = cut * per + i
            first, second = mix(part, f, level1, level1p, w_two, bit1)
            level2[f, :width, :rank] = first
            level2[f, :width, rank:] = -second
            level2[f, width:, :rank] = second
            level2[f, width:, rank:] = first
            return carry

        lax.fori_loop(0, per, body, 0)

    def outward(piece, t):
        at = pl.ds(pl.multiple_of(piece * rows + t * tile, tile), tile)
        w = jnp.concatenate(
            [w_out[f, c, at, :] for f in range(far) for c in range(2)], 1
        )
        x = jnp.concatenate([level2[f] for f in range(far)], 1)
        return dot_nt(x, w)

    def stage_e(part):
        def first_body(i, carry):
            high, t = i // tiles, lax.rem(i, tiles)
            value = outward(2 * high + 1 - bit0, t).astype(jnp.bfloat16)
            at = pl.ds(pl.multiple_of(t * tile, tile), tile)
            send1[part, high, 0, :, at] = value[:width]
            send1[part, high, 1, :, at] = value[width:]
            return carry

        lax.fori_loop(0, 2 * tiles, first_body, 0)
        copy = send(
            send1.at[part], recv1.at[part], r1_send.at[part], r1_recv.at[part], across0
        )

        def second_body(i, carry):
            high, t = i // tiles, lax.rem(i, tiles)
            value = outward(2 * high + bit0, t)
            at = pl.ds(pl.multiple_of(t * tile, tile), tile)
            held[part, high, 0, :, at] = value[:width]
            held[part, high, 1, :, at] = value[width:]
            return carry

        lax.fori_loop(0, 2 * tiles, second_body, 0)
        return copy

    def stage_f(part):
        away = held[part, 1 - bit1] + recv1[part, 1 - bit1].astype(jnp.float32)
        send2[part] = away.astype(jnp.bfloat16)
        copy = send(
            send2.at[part], recv2.at[part], r2_send.at[part], r2_recv.at[part], across1
        )
        near[part] += held[part, bit1] + recv1[part, bit1].astype(jnp.float32)
        return copy

    def stage_g(part):
        value = near[part] + recv2[part].astype(jnp.float32)
        out[:, part * width : (part + 1) * width, :] = value.astype(jnp.bfloat16)

    def near_field():
        has_before = jnp.where(flat > 0, 1, 0)
        has_after = jnp.where(flat < count - 1, 1, 0)

        def body(part, carry):
            at = pl.ds(pl.multiple_of(part * width, width), width)
            for i in range(leaves):
                real = jnp.zeros((width, leaf), jnp.float32)
                imag = jnp.zeros((width, leaf), jnp.float32)
                for offset in range(3):
                    j = i + offset - 1
                    weight = near_mask[i, offset]
                    if j < 0:
                        x = halo[0, :, at, :]
                        weight = weight * has_before
                    elif j >= leaves:
                        x = halo[1, :, at, :]
                        weight = weight * has_after
                    else:
                        x = arrived[group, :, at, j * leaf : (j + 1) * leaf]
                    product = dot_nt(
                        x.reshape(2 * width, leaf), w_near[i, offset].reshape(2 * leaf, leaf)
                    )
                    weight = weight.astype(jnp.float32)
                    real += weight * (product[:width, :leaf] - product[width:, leaf:])
                    imag += weight * (product[width:, :leaf] + product[:width, leaf:])
                near[part, 0, :, i * leaf : (i + 1) * leaf] = real
                near[part, 1, :, i * leaf : (i + 1) * leaf] = imag
            return carry

        lax.fori_loop(0, parts, body, 0)

    l0 = {}
    l1 = {}
    r1 = {}
    r2 = {}
    l0[0] = stage_a(0)
    if units > 1:
        l0[1] = stage_a(1)
    load_near.wait()
    for copy in halos:
        copy.wait_recv()
    near_field()
    load_one.wait()
    l0[0].wait_recv()
    l1[0] = stage_b(0)
    load_two.wait()
    load_out.wait()
    for unit in range(units):
        if unit + 2 < units:
            l0[unit + 2] = stage_a(unit + 2)
        if unit + 1 < units:
            l0[unit + 1].wait_recv()
            l1[unit + 1] = stage_b(unit + 1)
        l1[unit].wait_recv()
        stage_d(unit)
        part, cut = divmod(unit, cuts)
        if cut == cuts - 1:
            if part > 0:
                r1[part - 1].wait_recv()
                r2[part - 1] = stage_f(part - 1)
            r1[part] = stage_e(part)
    r1[parts - 1].wait_recv()
    r2[parts - 1] = stage_f(parts - 1)
    for part in range(parts):
        r2[part].wait_recv()
        stage_g(part)
    for copy in started:
        copy.wait_send()


def on_device(groups, members, *arrays):
    incident, near_blocks, near_mask, far_source, far_rank, basis_in, one, two, basis_out = arrays
    rhs, rows = incident.shape[1:]
    leaf = near_blocks.shape[3]
    far, _, rank = basis_in.shape[2:5]
    parts = PARTS
    cuts = CUTS if far % CUTS == 0 else 1
    width = rhs // parts
    units = parts * cuts
    bf16 = jnp.bfloat16
    dma = pltpu.SemaphoreType.DMA
    level = pltpu.VMEM((parts, far, 2, width, rank), bf16)
    sums = pltpu.VMEM((parts, 2, 2, width, rows), bf16)
    last = pltpu.VMEM((parts, 2, width, rows), bf16)
    somewhere = pl.BlockSpec(memory_space=pl.ANY)
    scalars = pl.BlockSpec(memory_space=pltpu.SMEM)
    return pl.pallas_call(
        functools.partial(kernel, groups, members),
        out_shape=jax.ShapeDtypeStruct(incident.shape, bf16),
        in_specs=[somewhere, somewhere, scalars, scalars, scalars] + [somewhere] * 4,
        out_specs=pl.BlockSpec(memory_space=pltpu.VMEM),
        scratch_shapes=[
            pltpu.VMEM((groups,) + incident.shape, bf16),
            pltpu.VMEM((2, 2, rhs, leaf), bf16),
            pltpu.VMEM(near_blocks.shape, bf16),
            pltpu.VMEM(basis_in.shape[2:], bf16),
            pltpu.VMEM(one.shape[2:], bf16),
            pltpu.VMEM(two.shape[2:], bf16),
            pltpu.VMEM(basis_out.shape[2:], bf16),
            level,
            level,
            level,
            level,
            pltpu.VMEM((far, 2 * width, 2 * rank), bf16),
            pltpu.VMEM((parts, 2, width, rows), jnp.float32),
            pltpu.VMEM((parts, 2, 2, width, rows), jnp.float32),
            sums,
            sums,
            last,
            last,
            dma((6,)),
            dma((2, groups)),
            dma((2, groups)),
            dma((2,)),
            dma((2,)),
            dma((units,)),
            dma((units,)),
            dma((units,)),
            dma((units,)),
            dma((parts,)),
            dma((parts,)),
            dma((parts,)),
            dma((parts,)),
        ],
        compiler_params=pltpu.CompilerParams(
            collective_id=0, has_side_effects=True, vmem_limit_bytes=62 * 1024 * 1024
        ),
    )(*arrays)


def solution(mesh):
    placed = (
        P(None, None, ("grp", "mem")),
        P(("grp", "mem"), None, None, None, None),
        P(("grp", "mem"), None),
        P(),
        P("grp", None),
        P("grp", "mem", None, None, None, None),
        P("grp", "mem", None, None, None, None),
        P("grp", "mem", None, None, None, None),
        P("grp", "mem", None, None, None, None),
    )
    return jax.shard_map(
        functools.partial(on_device, mesh.shape["grp"], mesh.shape["mem"]),
        mesh=mesh,
        in_specs=placed,
        out_specs=P(None, None, ("grp", "mem")),
        check_vma=False,
    )
```

time: 307 us -> 163 us (0.53)
  waiting for transfers between devices: 218 us -> 0 us
  Pallas kernels: 0 us -> 161 us
  local copies, waits for them, and re-layouts: 25.3 us -> 1.87 us
  matrix products: 22.3 us -> 0 us
  other arithmetic: 16.6 us -> 0 us
  between operations: 13.8 us -> 0.01 us
  starting transfers between devices: 9.92 us -> 0 us
    pallas_call x0 -> x1, Pallas kernels: none -> 161 us  [on_device(): pl.pallas_call(functools.partial(kernel, groups, members), out_shape=jax....]
    ppermute x4 -> x0, waiting for transfers between devices: 122 us -> none  [the longest x2 110 us: partner_2(): lax.ppermute(value, axis, [(i, i ^ 1 << stride) for i in range(lax.axis_s...]
    reduce_scatter x1 -> x0, waiting for transfers between devices: 59.6 us -> none  [on_device(): far = lax.psum_scatter(terms, 'mem', scatter_dimension=2, tiled=True)]
    all_gather x1 -> x0, waiting for transfers between devices: 35.6 us -> none  [on_device(): arrived = lax.all_gather(incident[None], 'grp', axis=0, tiled=True)]
    dot_general x28 -> x0, matrix products: 22.3 us -> none  [mult(): return jnp.einsum(form, left, right, preferred_element_type=jnp.float32)]
    unnamed x21 -> x1, local copies, waits for them, and re-layouts: 16.4 us -> 1.87 us
    ppermute x4 -> x0, starting transfers between devices: 9.88 us -> none  [the longest x1 4.56 us: with_halo(): lax.ppermute(lax.slice_in_dim(block, block.shape[dim] - width, None, axis...]
    select_n x4 -> x0, other arithmetic: 8.17 us -> none  [the longest x2 4.69 us: on_device(): chosen = jnp.take(arrived, sources, axis=0)]
  transfers between devices with their start and end apart: 6 -> 0, of which waited for: 6 -> 0; matrix products, arithmetic and copies ran while one was open for 7% -> 0% of each run, Pallas kernels for 0% -> 0%
where the time goes in v2:
time: 163 us
  Pallas kernels  161 us (99%)
  local copies, waits for them, and re-layouts  1.87 us (1%)
    pallas_call x1, Pallas kernels, on_device(): pl.pallas_call(functools.partial(kernel, groups, members), out_shape=jax....  161 us

profile of v2, /device:TPU:0, one launch (start us, length us, event | category | flops | bytes accessed | tf_op | source)
XLA Modules:
  0.0 162.7 jit_solution(5346340658931176822)
XLA Ops:
  0.0 160.9 %shard_map.91 = bf16[2,256,512]{2,1,0:T(8,128)(2,1)} custom-call(bf16[2,256,512]{2,1,0:T(8,128)(2,1)} %incident.1, bf16[2,3,2,256,256]{4,3,2,1,0:T(8,128)(2,1)} %near_blocks.1, s32[2,3]{1,0:T(2,128)} %near_mask.1, s32[8,14]{1,0:T(8,128)} %far_source.1, s32[1,14]{1,0:T(1,128)} %far_rank.1, bf16[1,1,14,2,128,512]{5,4,3,2,1,0:T(8,128)(2,1)} %basis_in.1, ...), custom_call_target="tpu_custom_call" | custom-call | tf_op jit(solution)/shard_map/pallas_call | solution.py:409
  160.9 1.9 %copy.11 = bf16[2,256,512]{2,1,0:T(8,128)(2,1)} copy(bf16[2,256,512]{2,1,0:T(8,128)(2,1)} %shard_map.91) | data formatting | bytes 1048576

commit v3 on v2

--- a/solution.py
+++ b/solution.py
@@ -31,7 +31,6 @@
     section_two,
     basis_out,
     out,
-    arrived,
     halo,
     w_near,
     w_in,
@@ -62,6 +61,7 @@
     r1_recv,
     r2_send,
     r2_recv,
+    *arrived,
 ):
     rhs, rows = incident.shape[1], incident.shape[2]
     leaves, leaf = near_blocks.shape[0], near_blocks.shape[3]
@@ -96,8 +96,14 @@
                 value = value + (1 - 2 * group_bits[b]) * (1 << b)
         return value
 
-    own = pltpu.make_async_copy(incident, arrived.at[group], load_sem.at[0])
-    own.start()
+    owns = [
+        pltpu.make_async_copy(
+            incident.at[:, pl.ds(part * width, width)], arrived[part].at[group], load_sem.at[5 + part]
+        )
+        for part in range(parts)
+    ]
+    for own in owns:
+        own.start()
     loads = []
     for i, (source, target) in enumerate(
         (
@@ -108,7 +114,7 @@
             (basis_out.at[0, 0], w_out),
         )
     ):
-        load = pltpu.make_async_copy(source, target, load_sem.at[i + 1])
+        load = pltpu.make_async_copy(source, target, load_sem.at[i])
         load.start()
         loads.append(load)
     load_in, load_near, load_one, load_two, load_out = loads
@@ -135,6 +141,61 @@
         started.append(copy)
         return copy
 
+    outer = list(range(1, bits))
+    orders = (outer, outer[::-1])
+    number = {}
+    masks = {}
+    sideways = {}
+    pending = {}
+
+    def pass_on(part, half, mask, bit):
+        at = pl.ds(part * width, width)
+        slot = arrived[part].at[flipped(mask), half]
+        j = number.get((part, half), 0)
+        number[part, half] = j + 1
+        return send(
+            incident.at[half, at] if mask == 0 else slot,
+            slot,
+            gather_send.at[part, half, j],
+            gather_recv.at[part, half, j],
+            {"grp": flipped(1 << bit)},
+        )
+
+    def gather(part, stage):
+        if part >= parts or stage > len(outer):
+            return
+        for half in range(2):
+            if stage == 0:
+                masks[part, half] = [0]
+                fresh = [0]
+            else:
+                for copy in pending[part, half]:
+                    copy.wait_recv()
+                fresh = [mask ^ 1 << orders[half][stage - 1] for mask in masks[part, half]]
+                masks[part, half] = masks[part, half] + fresh
+            if stage < len(outer):
+                pending[part, half] = [
+                    pass_on(part, half, mask, orders[half][stage]) for mask in masks[part, half]
+                ]
+            sideways.setdefault(part, []).extend(pass_on(part, half, mask, 0) for mask in fresh)
+
+    def gathered(part):
+        for stage in range(progress[part], len(outer) + 1):
+            gather(part, stage)
+        progress[part] = len(outer) + 1
+        for copy in sideways.pop(part):
+            copy.wait_recv()
+
+    progress = [0] * parts
+
+    def advance():
+        for part in reversed(range(parts)):
+            before_it = progress[part - 1] if part else len(outer) + 1
+            if progress[part] <= len(outer) and progress[part] < before_it:
+                gather(part, progress[part])
+                progress[part] += 1
+
+    advance()
     halos = [
         send(
             incident.at[:, :, pl.ds(rows - leaf, leaf)],
@@ -152,44 +213,10 @@
         ),
     ]
 
-    own.wait()
-    outer = list(range(1, bits))
-    orders = (outer, outer[::-1])
-    number = [0, 0]
-
-    def pass_on(half, mask, bit):
-        slot = arrived.at[flipped(mask), half]
-        j = number[half]
-        number[half] += 1
-        return send(
-            slot, slot, gather_send.at[half, j], gather_recv.at[half, j], {"grp": flipped(1 << bit)}
-        )
-
-    masks = [[0], [0]]
-    sideways = []
-    pending = []
-    for half in range(2):
-        if outer:
-            pending.append((half, [pass_on(half, 0, orders[half][0])]))
-    for half in range(2):
-        sideways.append(pass_on(half, 0, 0))
-    for stage in range(len(outer)):
-        later = []
-        for half, copies in pending:
-            for copy in copies:
-                copy.wait_recv()
-            fresh = [mask ^ 1 << orders[half][stage] for mask in masks[half]]
-            masks[half] = masks[half] + fresh
-            if stage + 1 < len(outer):
-                later.append(
-                    (half, [pass_on(half, mask, orders[half][stage + 1]) for mask in masks[half]])
-                )
-            for mask in fresh:
-                sideways.append(pass_on(half, mask, 0))
-        pending = later
+    for own in owns:
+        own.wait()
+    advance()
     load_in.wait()
-    for copy in sideways:
-        copy.wait_recv()
 
     def combine(product):
         first = product[:width, :rank] - product[width:, rank:]
@@ -205,7 +232,7 @@
 
         def body(i, carry):
             f = cut * per + i
-            x = arrived[far_source[group, f], :, part * width : (part + 1) * width, :]
+            x = arrived[part][far_source[group, f]]
             first, second = combine(
                 dot_nt(x.reshape(2 * width, rows), w_in[f].reshape(2 * rank, rows))
             )
@@ -281,39 +308,42 @@
         x = jnp.concatenate([level2[f] for f in range(far)], 1)
         return dot_nt(x, w)
 
-    def stage_e(part):
-        def first_body(i, carry):
-            high, t = i // tiles, lax.rem(i, tiles)
+    def send_first(part, high, index):
+        def body(t, carry):
             value = outward(2 * high + 1 - bit0, t).astype(jnp.bfloat16)
             at = pl.ds(pl.multiple_of(t * tile, tile), tile)
             send1[part, high, 0, :, at] = value[:width]
             send1[part, high, 1, :, at] = value[width:]
             return carry
 
-        lax.fori_loop(0, 2 * tiles, first_body, 0)
-        copy = send(
-            send1.at[part], recv1.at[part], r1_send.at[part], r1_recv.at[part], across0
-        )
-
-        def second_body(i, carry):
-            high, t = i // tiles, lax.rem(i, tiles)
+        lax.fori_loop(0, tiles, body, 0)
+        return send(
+            send1.at[part, high],
+            recv1.at[part, high],
+            r1_send.at[2 * part + index],
+            r1_recv.at[2 * part + index],
+            across0,
+        )
+
+    def hold(part, high):
+        def body(t, carry):
             value = outward(2 * high + bit0, t)
             at = pl.ds(pl.multiple_of(t * tile, tile), tile)
             held[part, high, 0, :, at] = value[:width]
             held[part, high, 1, :, at] = value[width:]
             return carry
 
-        lax.fori_loop(0, 2 * tiles, second_body, 0)
-        return copy
-
-    def stage_f(part):
+        lax.fori_loop(0, tiles, body, 0)
+
+    def send_second(part):
         away = held[part, 1 - bit1] + recv1[part, 1 - bit1].astype(jnp.float32)
         send2[part] = away.astype(jnp.bfloat16)
-        copy = send(
+        return send(
             send2.at[part], recv2.at[part], r2_send.at[part], r2_recv.at[part], across1
         )
+
+    def add_first(part):
         near[part] += held[part, bit1] + recv1[part, bit1].astype(jnp.float32)
-        return copy
 
     def stage_g(part):
         value = near[part] + recv2[part].astype(jnp.float32)
@@ -323,8 +353,8 @@
         has_before = jnp.where(flat > 0, 1, 0)
         has_after = jnp.where(flat < count - 1, 1, 0)
 
-        def body(part, carry):
-            at = pl.ds(pl.multiple_of(part * width, width), width)
+        for part in range(parts):
+            at = pl.ds(part * width, width)
             for i in range(leaves):
                 real = jnp.zeros((width, leaf), jnp.float32)
                 imag = jnp.zeros((width, leaf), jnp.float32)
@@ -338,7 +368,7 @@
                         x = halo[1, :, at, :]
                         weight = weight * has_after
                     else:
-                        x = arrived[group, :, at, j * leaf : (j + 1) * leaf]
+                        x = arrived[part][group, :, :, j * leaf : (j + 1) * leaf]
                     product = dot_nt(
                         x.reshape(2 * width, leaf), w_near[i, offset].reshape(2 * leaf, leaf)
                     )
@@ -347,29 +377,39 @@
                     imag += weight * (product[width:, :leaf] + product[:width, leaf:])
                 near[part, 0, :, i * leaf : (i + 1) * leaf] = real
                 near[part, 1, :, i * leaf : (i + 1) * leaf] = imag
-            return carry
-
-        lax.fori_loop(0, parts, body, 0)
 
     l0 = {}
     l1 = {}
     r1 = {}
     r2 = {}
-    l0[0] = stage_a(0)
-    if units > 1:
-        l0[1] = stage_a(1)
+
+    def start_a(unit):
+        if unit < units:
+            if unit % cuts == 0:
+                gathered(unit // cuts)
+            l0[unit] = stage_a(unit)
+
+    def second(part):
+        r1[part][0].wait_recv()
+        r2[part] = send_second(part)
+
+    start_a(0)
+    advance()
+    start_a(1)
+    advance()
     load_near.wait()
+    load_one.wait()
+    l0[0].wait_recv()
+    l1[0] = stage_b(0)
+    advance()
     for copy in halos:
         copy.wait_recv()
     near_field()
-    load_one.wait()
-    l0[0].wait_recv()
-    l1[0] = stage_b(0)
     load_two.wait()
     load_out.wait()
     for unit in range(units):
-        if unit + 2 < units:
-            l0[unit + 2] = stage_a(unit + 2)
+        advance()
+        start_a(unit + 2)
         if unit + 1 < units:
             l0[unit + 1].wait_recv()
             l1[unit + 1] = stage_b(unit + 1)
@@ -377,13 +417,21 @@
         stage_d(unit)
         part, cut = divmod(unit, cuts)
         if cut == cuts - 1:
+            r1[part] = (send_first(part, 1 - bit1, 0), send_first(part, bit1, 1))
+            hold(part, 1 - bit1)
             if part > 0:
-                r1[part - 1].wait_recv()
-                r2[part - 1] = stage_f(part - 1)
-            r1[part] = stage_e(part)
-    r1[parts - 1].wait_recv()
-    r2[parts - 1] = stage_f(parts - 1)
-    for part in range(parts):
+                second(part - 1)
+                r1[part - 1][1].wait_recv()
+                add_first(part - 1)
+            if part == parts - 1:
+                second(part)
+            hold(part, bit1)
+            if part > 1:
+                r2[part - 2].wait_recv()
+                stage_g(part - 2)
+    r1[parts - 1][1].wait_recv()
+    add_first(parts - 1)
+    for part in range(max(parts - 2, 0), parts):
         r2[part].wait_recv()
         stage_g(part)
     for copy in started:
@@ -412,7 +460,6 @@
         in_specs=[somewhere, somewhere, scalars, scalars, scalars] + [somewhere] * 4,
         out_specs=pl.BlockSpec(memory_space=pltpu.VMEM),
         scratch_shapes=[
-            pltpu.VMEM((groups,) + incident.shape, bf16),
             pltpu.VMEM((2, 2, rhs, leaf), bf16),
             pltpu.VMEM(near_blocks.shape, bf16),
             pltpu.VMEM(basis_in.shape[2:], bf16),
@@ -430,20 +477,21 @@
             sums,
             last,
             last,
-            dma((6,)),
-            dma((2, groups)),
-            dma((2, groups)),
+            dma((5 + parts,)),
+            dma((parts, 2, 2 * groups)),
+            dma((parts, 2, 2 * groups)),
             dma((2,)),
             dma((2,)),
             dma((units,)),
             dma((units,)),
             dma((units,)),
             dma((units,)),
+            dma((2 * parts,)),
+            dma((2 * parts,)),
             dma((parts,)),
             dma((parts,)),
-            dma((parts,)),
-            dma((parts,)),
-        ],
+        ]
+        + [pltpu.VMEM((groups, 2, width, rows), bf16)] * parts,
         compiler_params=pltpu.CompilerParams(
             collective_id=0, has_side_effects=True, vmem_limit_bytes=62 * 1024 * 1024
         ),

time: 163 us -> 153 us (0.939)
  Pallas kernels: 161 us -> 151 us
    pallas_call x1, Pallas kernels: 161 us -> 151 us  [on_device(): pl.pallas_call(functools.partial(kernel, groups, members), out_shape=jax....]
where the time goes in v3:
time: 153 us
  Pallas kernels  151 us (99%)
  local copies, waits for them, and re-layouts  1.87 us (1%)
    pallas_call x1, Pallas kernels, on_device(): pl.pallas_call(functools.partial(kernel, groups, members), out_shape=jax....  151 us

profile of v3, /device:TPU:0, one launch (start us, length us, event | category | flops | bytes accessed | tf_op | source)
XLA Modules:
  0.0 153.2 jit_solution(16701979821179344444)
XLA Ops:
  0.0 151.4 %shard_map.91 = bf16[2,256,512]{2,1,0:T(8,128)(2,1)} custom-call(bf16[2,256,512]{2,1,0:T(8,128)(2,1)} %incident.1, bf16[2,3,2,256,256]{4,3,2,1,0:T(8,128)(2,1)} %near_blocks.1, s32[2,3]{1,0:T(2,128)} %near_mask.1, s32[8,14]{1,0:T(8,128)} %far_source.1, s32[1,14]{1,0:T(1,128)} %far_rank.1, bf16[1,1,14,2,128,512]{5,4,3,2,1,0:T(8,128)(2,1)} %basis_in.1, ...), custom_call_target="tpu_custom_call" | custom-call | tf_op jit(solution)/shard_map/pallas_call | solution.py:457
  151.4 1.9 %copy.11 = bf16[2,256,512]{2,1,0:T(8,128)(2,1)} copy(bf16[2,256,512]{2,1,0:T(8,128)(2,1)} %shard_map.91) | data formatting | bytes 1048576

commit v4 on v3

--- a/solution.py
+++ b/solution.py
@@ -9,7 +9,7 @@
 
 MESH = pl.DeviceIdType.MESH
 PARTS = 4
-CUTS = 2
+CUTS = 1
 
 
 def dot_nt(left, right):

time: 153 us -> 150 us (0.980)
  Pallas kernels: 151 us -> 147 us
    pallas_call x1, Pallas kernels: 151 us -> 147 us  [on_device(): pl.pallas_call(functools.partial(kernel, groups, members), out_shape=jax....]
where the time goes in v4:
time: 150 us; the launch traced here: 149 us
  Pallas kernels  147 us (98%)
  local copies, waits for them, and re-layouts  1.87 us (1%)
    pallas_call x1, Pallas kernels, on_device(): pl.pallas_call(functools.partial(kernel, groups, members), out_shape=jax....  147 us

profile of v4, /device:TPU:0, one launch (start us, length us, event | category | flops | bytes accessed | tf_op | source)
XLA Modules:
  0.0 149.4 jit_solution(7040862866725957783)
XLA Ops:
  0.0 147.5 %shard_map.91 = bf16[2,256,512]{2,1,0:T(8,128)(2,1)} custom-call(bf16[2,256,512]{2,1,0:T(8,128)(2,1)} %incident.1, bf16[2,3,2,256,256]{4,3,2,1,0:T(8,128)(2,1)} %near_blocks.1, s32[2,3]{1,0:T(2,128)} %near_mask.1, s32[8,14]{1,0:T(8,128)} %far_source.1, s32[1,14]{1,0:T(1,128)} %far_rank.1, bf16[1,1,14,2,128,512]{5,4,3,2,1,0:T(8,128)(2,1)} %basis_in.1, ...), custom_call_target="tpu_custom_call" | custom-call | tf_op jit(solution)/shard_map/pallas_call | solution.py:457
  147.5 1.9 %copy.11 = bf16[2,256,512]{2,1,0:T(8,128)(2,1)} copy(bf16[2,256,512]{2,1,0:T(8,128)(2,1)} %shard_map.91) | data formatting | bytes 1048576
